TPU v7x, 32 devices: a whole 2x2x4 slice. The times are simulated.
32 devices in a mesh: section: 4 (over x, core), dp: 8 (over z, y).
Axes of the slice: x: 2, y: 2, z: 4, core: 2. Of those that a mesh axis runs over, the one named last changes fastest.
Arguments:
- acts: bfloat16 [4, 3072, 4096], P('section', 'dp'), may hold values from -6 to 6
- cotangent: bfloat16 [3072, 4096], P('dp'), may hold values from -6 to 6
- gains: float32 [4, 4096], P('section'), may hold values from 0.1 to 1.9
- value_w: bfloat16 [4, 4096, 1024], P('section', 'dp'), may hold values from -0.09375 to 0.09375
- output_w: bfloat16 [4, 1024, 4096], P('section', None, 'dp'), may hold values from -0.1875 to 0.1875
- d_map: int32 [4, 64], P('section'), may hold values from 0 to 3
- r_map: int32 [4, 16], P('section'), may hold values from 0 to 3
- lengths: int32 [24], P('dp'), may hold values from 32 to 128, as said below
- item_panels: bfloat16 [8, 4, 2, 128, 128], P('dp', 'section'), may hold values from -24 to 24
- owners: int32 [8], replicated, may hold values from 0 to 7, each once
Outputs:
- grad_in: bfloat16 [4, 3072, 4096], P('section', 'dp')
- scores: float32 [24, 8], P('dp')
Inputs may be any that keep to these rules, and one draw needn't show every extreme that they name: `lengths`: some document is fully live (128 tokens) in every draw.
All inputs are finite; a program needn't handle non-finite values.
Results may differ from a plain program's by a relative error of at most 0.015.
Values may be sent and summed in bfloat16 or wider, within the bound.
A program may use at most 128 MiB of HBM per device.

v0:
```python
import jax
import jax.numpy as jnp
from jax import lax
from jax.sharding import PartitionSpec as P

BLOCK = 64
DBINS = 2
RBINS = 2


def shifted(block, axis, distance):
    devices = range(lax.axis_size(axis))
    route = [(i - distance, i) for i in devices if i - distance in devices]
    return lax.ppermute(block, axis, route)


def normalize(inputs, gain_row):
    return inputs * lax.rsqrt(jnp.mean(inputs * inputs, axis=-1, keepdims=True) + 1e-05) * gain_row


def sketch_matrix(codes, bin_count):
    levels = jnp.arange(bin_count, dtype=jnp.int32)
    sign_row = (1 - 2 * (codes // bin_count)).astype(jnp.bfloat16)
    return jnp.where(
        levels[:, None] == (codes % bin_count)[None, :],
        sign_row[None, :],
        jnp.zeros_like(sign_row)[None, :],
    )


def project_rows(values, sketch):
    row_count = values.shape[0]
    block_count = values.shape[1] // BLOCK
    bin_count = sketch.shape[0]
    pieces = values.reshape(row_count, block_count, BLOCK)
    mapped = jnp.einsum("tbc,kb->tkc", pieces, sketch, preferred_element_type=jnp.float32)
    return mapped.reshape(row_count, bin_count * BLOCK) * (block_count / bin_count) ** (-0.5)


def section_work(
    inputs_bf, current, gain_row, value_full, output_full, model_sketch, value_sketch, doc_lens
):
    row_count = inputs_bf.shape[0]
    doc_count = doc_lens.shape[0]
    slot_count = row_count // doc_count
    inputs = inputs_bf.astype(jnp.float32)
    hidden = normalize(inputs, gain_row).astype(jnp.bfloat16)
    values = jnp.dot(hidden, value_full, preferred_element_type=jnp.float32).astype(jnp.bfloat16)
    dvalues = lax.dot_general(
        current, output_full, (((1,), (1,)), ((), ())), preferred_element_type=jnp.float32
    ).astype(jnp.bfloat16)
    dhidden = lax.dot_general(
        dvalues, value_full, (((1,), (1,)), ((), ())), preferred_element_type=jnp.float32
    )
    _, pullback = jax.vjp(lambda probe: normalize(probe, gain_row), inputs)
    grad_next = (current.astype(jnp.float32) + pullback(dhidden)[0]).astype(jnp.bfloat16)
    hidden_proj = project_rows(hidden, model_sketch).reshape(doc_count, slot_count, -1)
    dvalue_proj = project_rows(dvalues, value_sketch).reshape(doc_count, slot_count, -1)
    grad_proj = project_rows(current, model_sketch).reshape(doc_count, slot_count, -1)
    value_proj = project_rows(values, value_sketch).reshape(doc_count, slot_count, -1)
    first_feat = jnp.einsum(
        "dtk,dtj->dkj", hidden_proj, dvalue_proj, precision=lax.Precision.HIGHEST
    )
    second_feat = jnp.einsum("dtk,dtj->dkj", grad_proj, value_proj, precision=lax.Precision.HIGHEST)
    inverse_len = 1.0 / doc_lens.astype(jnp.float32)
    features = jnp.stack([first_feat, second_feat], axis=1) * inverse_len[:, None, None, None]
    return (grad_next, features.reshape(doc_count, -1))


def body(acts, cotangent, gains, value_w, output_w, d_map, r_map, lengths, item_panels, owners):
    section_count = lax.axis_size("section")
    section_id = lax.axis_index("section")
    last_section = section_count - 1
    value_full, output_full = (
        lax.all_gather(value_w[0], "dp", axis=0, tiled=True),
        lax.all_gather(output_w[0], "dp", axis=1, tiled=True),
    )
    model_sketch = sketch_matrix(d_map[0], DBINS)
    value_sketch = sketch_matrix(r_map[0], RBINS)
    gain_row = gains[0]
    layer_inputs = acts[0]
    token_count = layer_inputs.shape[0]
    model_width = layer_inputs.shape[1]
    doc_count = lengths.shape[0]
    slot_count = token_count // doc_count
    feature_width = item_panels.shape[2] * item_panels.shape[3] * item_panels.shape[4]
    group_count = 1
    group_rows = token_count // group_count
    positions = jnp.arange(slot_count, dtype=jnp.int32)

    def advance(turn, carry):
        incoming, grad_store, feat_store = carry
        group_id = turn - (last_section - section_id)
        is_live = (group_id >= 0) & (group_id < group_count)
        cot_rows = cotangent
        live_mask = (positions[None, :] < lengths[:, None]).reshape(group_rows, 1)
        cot_rows = jnp.where(live_mask, cot_rows, jnp.zeros_like(cot_rows))
        current = jnp.where(section_id == last_section, cot_rows, incoming)

        def active(stores):
            grad_next, features = section_work(
                layer_inputs,
                current,
                gain_row,
                value_full,
                output_full,
                model_sketch,
                value_sketch,
                lengths,
            )
            return (grad_next, grad_next, features)

        def resting(stores):
            return (jnp.zeros_like(incoming), stores[0], stores[1])

        outgoing, grad_store, feat_store = lax.cond(
            is_live, active, resting, (grad_store, feat_store)
        )
        incoming = shifted(outgoing, "section", -1)
        return (incoming, grad_store, feat_store)

    start_state = (
        jnp.zeros((group_rows, model_width), jnp.bfloat16),
        jnp.zeros((token_count, model_width), jnp.bfloat16),
        jnp.zeros((doc_count, feature_width), jnp.float32),
    )
    _, grad_store, feat_store = lax.fori_loop(
        0, section_count + group_count - 1, advance, start_state
    )
    features = feat_store.astype(jnp.bfloat16)
    own_panels = item_panels[:, 0].reshape(item_panels.shape[0], feature_width)
    per_owner = own_panels.shape[0]
    owner_count = lax.axis_size("dp")
    all_rows = lax.all_gather(own_panels, "dp", axis=0, tiled=True)
    products = lax.dot_general(
        features, all_rows, (((1,), (1,)), ((), ())), preferred_element_type=jnp.float32
    )
    collected = jnp.take(
        products.reshape(doc_count, owner_count, per_owner), owners, axis=1
    ).reshape(doc_count, owner_count * per_owner)
    scaled = collected * (feature_width // 2) ** (-0.5)
    scores = lax.psum(scaled, "section")
    return (grad_store[None], scores)


def solution(mesh):
    in_specs = (
        P("section", "dp", None),
        P("dp", None),
        P("section", None),
        P("section", "dp", None),
        P("section", None, "dp"),
        P("section", None),
        P("section", None),
        P("dp"),
        P("dp", "section", None, None, None),
        P(),
    )
    out_specs = (P("section", "dp", None), P("dp", None))
    return jax.shard_map(body, mesh=mesh, in_specs=in_specs, out_specs=out_specs, check_vma=False)
```

profile of v0, /device:TPU:0, one launch (start us, length us, event | category | flops | bytes accessed | tf_op | source)
XLA Modules:
  0.0 611.6 jit_solution(2032580142594730946)
XLA Ops:
  14.5 40.6 %all-gather.2 = bf16[8,1,32768]{2,1,0:T(2,128)(2,1)} all-gather(bf16[1,1,32768]{2,1,0:T(2,128)(2,1)S(1)} %reshape.128), channel_id=1, replica_groups=mesh['section'=4,'dp'=8] {'dp'}, dimensions={0}, use_global_device_ids=true | all-gather | bytes 589824 | tf_op jit(solution)/shard_map/all_gather | solution.py:134
  55.1 91.4 %all-gather.8.cloned.1.call-done = bf16[1,4096,1024]{2,1,0:T(8,128)(2,1)} async-done(((bf16[1,512,1024]{2,1,0:T(8,128)(2,1)}), bf16[1,4096,1024]{2,1,0:T(8,128)(2,1)}) %all-gather.8.cloned.1.call-update) | async-done | bytes 8388624 | tf_op jit(solution)/shard_map/all_gather | solution.py:75
  146.5 125.6 %all-gather.6.cloned.1.call-done = bf16[1,1024,4096]{2,1,0:T(8,128)(2,1)} async-done(((bf16[1,1024,512]{2,1,0:T(8,128)(2,1)}), bf16[1,1024,4096]{2,1,0:T(8,128)(2,1)}) %all-gather.6.cloned.1.call-update) | async-done | bytes 8388624 | tf_op jit(solution)/shard_map/all_gather | solution.py:76
  277.0 316.0 %while.20 = (s32[]{:T(128)}, bf16[384,4096]{1,0:T(8,128)(2,1)}, bf16[384,4096]{1,0:T(8,128)(2,1)}, bf16[3,32768]{1,0:T(4,128)(2,1)}, s32[]{:T(128)}, /*index=5*/...) while((s32[]{:T(128)}, bf16[384,4096]{1,0:T(8,128)(2,1)}, ...), condition=%wide.region_5.6_spmd.clone, body=%wide.region_0.5_spmd.clone.sunk | while | flops 9861564416 | bytes 193448656 | solution.py:127
  277.0 2.1 conditional.3
  277.0 2.1 broadcast.174
  280.4 6.5 %collective-permute-done = bf16[384,4096]{1,0:T(8,128)(2,1)S(1)} collective-permute-done((bf16[384,4096]{1,0:T(8,128)(2,1)}, bf16[384,4096]{1,0:T(8,128)(2,1)S(1)}, u32[]{:S(2)}, u32[]{:S(2)}) %collective-permute-start) | collective-permute-done | bytes 3145760 | tf_op jit(solution)/shard_map/while/body/eval_jaxpr/ppermute | solution.py:14
  288.5 2.1 conditional.3
  291.9 36.9 %collective-permute-done = bf16[384,4096]{1,0:T(8,128)(2,1)S(1)} collective-permute-done((bf16[384,4096]{1,0:T(8,128)(2,1)}, bf16[384,4096]{1,0:T(8,128)(2,1)S(1)}, u32[]{:S(2)}, u32[]{:S(2)}) %collective-permute-start) | collective-permute-done | bytes 3145760 | tf_op jit(solution)/shard_map/while/body/eval_jaxpr/ppermute | solution.py:14
  333.8 185.5 %collective-permute-done = bf16[384,4096]{1,0:T(8,128)(2,1)S(1)} collective-permute-done((bf16[384,4096]{1,0:T(8,128)(2,1)}, bf16[384,4096]{1,0:T(8,128)(2,1)S(1)}, u32[]{:S(2)}, u32[]{:S(2)}) %collective-permute-start) | collective-permute-done | bytes 3145760 | tf_op jit(solution)/shard_map/while/body/eval_jaxpr/ppermute | solution.py:14
  521.0 62.6 %conditional.3 = (bf16[384,4096]{1,0:T(8,128)(2,1)}, bf16[384,4096]{1,0:T(8,128)(2,1)}, bf16[3,32768]{1,0:T(4,128)(2,1)}) conditional(s32[]{:T(128)} %convert_element_type.77, (bf16[384,4096]{1,0:T(8,128)(2,1)}, bf16[3,32768]{1,0:T(4,128)(2,1)}) %tuple.72, (pred[]{:T(512)}, s32[128]{0:T(128)S(1)}, s32[3]{0:T(128)}, bf16[384,4096]{1,0:T(8,128)(2,1)}, ...), branch_computations={%region_1.1_spmd, %region_2.4_spmd} | conditional | flops 9861564416 | bytes 168281216 | solution.py:116
  524.7 3.4 select_select_fusion
  529.9 4.3 convolution_convert_fusion.1
  534.3 2.3 copy.40
  536.6 2.3 fusion.22
  541.0 2.8 copy.45
  543.8 3.7 fusion.24
  549.2 8.4 %fusion.8 = (f32[384]{0:T(512)S(1)}, f32[384]{0:T(512)S(1)}, f32[384,4096]{1,0:T(8,128)S(1)}) fusion(bf16[384,4096]{1,0:T(8,128)(2,1)} %get-tuple-element.386, f32[4096]{0:T(1024)S(1)} %bitcast.69, bf16[384,1024]{1,0:T(8,128)(2,1)} %convolution_convert_fusion.1, bf16[4096,1024]{1,0:T(8,128)(2,1)} %get-tuple-element.384), kind=kOutput, calls=%fused_computation.11 | convolution fusion | flops 3230661632 | bytes 18631680 | tf_op jit(solution)/shard_map/while/body/eval_jaxpr/cond/branch_1_fun/dot_general | solution.py:52
  557.6 3.9 fusion.11
  563.2 6.8 %convolution_convert_fusion = bf16[384,1024]{1,0:T(8,128)(2,1)} fusion(bf16[384,4096]{1,0:T(8,128)(2,1)S(1)} %get-tuple-element.513, bf16[4096,1024]{1,0:T(8,128)(2,1)} %get-tuple-element.384), kind=kOutput, calls=%fused_computation.21 | convolution fusion | flops 3221618688 | bytes 12320768 | tf_op jit(solution)/shard_map/while/body/eval_jaxpr/cond/branch_1_fun/dot_general | solution.py:48
  570.0 3.4 copy.37
  579.7 3.9 copy.92
  584.9 6.5 %collective-permute-done = bf16[384,4096]{1,0:T(8,128)(2,1)S(1)} collective-permute-done((bf16[384,4096]{1,0:T(8,128)(2,1)}, bf16[384,4096]{1,0:T(8,128)(2,1)S(1)}, u32[]{:S(2)}, u32[]{:S(2)}) %collective-permute-start) | collective-permute-done | bytes 3145760 | tf_op jit(solution)/shard_map/while/body/eval_jaxpr/ppermute | solution.py:14
  596.5 7.6 %psum.7 = f32[3,8]{0,1:T(8,128)S(1)} all-reduce(f32[3,8]{0,1:T(8,128)S(1)} %multiply_bitcast_fusion), channel_id=1, replica_groups=mesh['section'=4,'dp'=8] {'section'}, use_global_device_ids=true, to_apply=%region_6.7 | all-reduce | flops 24 | bytes 192 | tf_op jit(solution)/shard_map/psum | solution.py:142
  (83 shorter events, 51.4 us)
Async XLA Ops:
  7.2 139.4 %all-gather.8.cloned.1.call-start = ((), (), s32[]{:S(2)}) async-start(), calls=%async_computation.1 | async-start | bytes 9437184 | tf_op jit(solution)/shard_map/all_gather | solution.py:75
  7.9 264.3 %all-gather.6.cloned.1.call-start = ((), (), s32[]{:S(2)}) async-start(), calls=%async_computation | async-start | bytes 9437184 | tf_op jit(solution)/shard_map/all_gather | solution.py:76
  273.0 4.1 copy-start.4
  279.1 7.8 %collective-permute-start = (bf16[384,4096]{1,0:T(8,128)(2,1)}, bf16[384,4096]{1,0:T(8,128)(2,1)S(1)}, u32[]{:S(2)}, u32[]{:S(2)}) collective-permute-start(bf16[384,4096]{1,0:T(8,128)(2,1)} %get-tuple-element.622), channel_id=1, source_target_pairs={{8,0},{16,8},{24,16},{9,1},{17,9},{25,17},{10,2},{18,10},{26,18},{... | collective-permute-start | bytes 9437192 | tf_op jit(solution)/shard_map/while/body/eval_jaxpr/ppermute | solution.py:14
  286.9 1.6 copy-start.1
  290.6 38.1 %collective-permute-start = (bf16[384,4096]{1,0:T(8,128)(2,1)}, bf16[384,4096]{1,0:T(8,128)(2,1)S(1)}, u32[]{:S(2)}, u32[]{:S(2)}) collective-permute-start(bf16[384,4096]{1,0:T(8,128)(2,1)} %get-tuple-element.622), channel_id=1, source_target_pairs={{8,0},{16,8},{24,16},{9,1},{17,9},{25,17},{10,2},{18,10},{26,18},{... | collective-permute-start | bytes 9437192 | tf_op jit(solution)/shard_map/while/body/eval_jaxpr/ppermute | solution.py:14
  328.8 1.6 copy-start.1
  332.5 186.8 %collective-permute-start = (bf16[384,4096]{1,0:T(8,128)(2,1)}, bf16[384,4096]{1,0:T(8,128)(2,1)S(1)}, u32[]{:S(2)}, u32[]{:S(2)}) collective-permute-start(bf16[384,4096]{1,0:T(8,128)(2,1)} %get-tuple-element.622), channel_id=1, source_target_pairs={{8,0},{16,8},{24,16},{9,1},{17,9},{25,17},{10,2},{18,10},{26,18},{... | collective-permute-start | bytes 9437192 | tf_op jit(solution)/shard_map/while/body/eval_jaxpr/ppermute | solution.py:14
  519.3 1.6 copy-start.1
  523.5 13.1 %copy-start.5 = (bf16[2,16,1]{1,0,2:T(2,128)(2,1)}, bf16[2,16,1]{1,0,2:T(2,128)(2,1)S(1)}, u32[]{:S(2)}) copy-start(bf16[2,16,1]{1,0,2:T(2,128)(2,1)S(1)} %fusion.36) | copy-start | bytes 196 | tf_op jit(solution)/shard_map/while/body/eval_jaxpr/cond
  524.7 5.2 copy-start.9
  541.0 2.8 copy-start.7
  549.2 8.4 %copy-start.2 = (bf16[384,4096]{1,0:T(8,128)(2,1)S(1)}, bf16[384,4096]{1,0:T(8,128)(2,1)}, u32[]{:S(2)}) copy-start(bf16[384,4096]{1,0:T(8,128)(2,1)} %get-tuple-element.386) | copy-start | bytes 9437188 | tf_op jit(solution)/shard_map/while/body/eval_jaxpr/cond
  561.5 1.7 copy-start
  573.4 3.4 copy-start.6
  575.2 2.2 copy-start.3
  576.8 1.9 copy-start.8
  583.6 7.8 %collective-permute-start = (bf16[384,4096]{1,0:T(8,128)(2,1)}, bf16[384,4096]{1,0:T(8,128)(2,1)S(1)}, u32[]{:S(2)}, u32[]{:S(2)}) collective-permute-start(bf16[384,4096]{1,0:T(8,128)(2,1)} %get-tuple-element.622), channel_id=1, source_target_pairs={{8,0},{16,8},{24,16},{9,1},{17,9},{25,17},{10,2},{18,10},{26,18},{... | collective-permute-start | bytes 9437192 | tf_op jit(solution)/shard_map/while/body/eval_jaxpr/ppermute | solution.py:14
  591.3 1.6 copy-start.1
Sparse Core Ops, SparseCore 0:
  10.1 136.3 all-gather.7
  148.6 123.5 all-gather.5
where the time goes:
time: 612 us
  waiting for transfers between devices  454 us (74%)
  blocking collectives  48.3 us (8%)
  local copies, waits for them, and re-layouts  41.7 us (7%)
  matrix products  30.7 us (5%)
  other arithmetic  17.7 us (3%)
  between operations  14.1 us (2%)
    ppermute x4, waiting for transfers between devices, shifted(): return lax.ppermute(block, axis, route)  235 us
    all_gather x1, waiting for transfers between devices, body(): lax.all_gather(output_w[0], 'dp', axis=1, tiled=True)  126 us
    all_gather x1, waiting for transfers between devices, body(): lax.all_gather(value_w[0], 'dp', axis=0, tiled=True)  91.4 us
    all_gather x1, blocking collectives, body(): all_rows = lax.all_gather(own_panels, 'dp', axis=0, tiled=True)  40.6 us
  transfers between devices with their start and end apart: 6, of which 6 were waited for; matrix products, arithmetic and copies ran while one was open for 1% of the time, Pallas kernels for 0%

commit v1 on v0

v1 whole, which is shorter than its diff:
```python
import jax
import jax.numpy as jnp
from jax import lax
from jax.sharding import PartitionSpec as P

BLOCK = 64
DBINS = 2
RBINS = 2
EPS = 1e-05


def projection(codes, bin_count):
    width = codes.shape[0] * BLOCK
    row_codes = jnp.repeat(codes, BLOCK)[:, None]
    shape = (width, bin_count * BLOCK)
    rows = lax.broadcasted_iota(jnp.int32, shape, 0)
    cols = lax.broadcasted_iota(jnp.int32, shape, 1)
    hit = (rows % BLOCK == cols % BLOCK) & (row_codes % bin_count == cols // BLOCK)
    sign = 1 - 2 * (row_codes // bin_count)
    return jnp.where(hit, sign, 0).astype(jnp.bfloat16)


def project_rows(values, matrix, bin_count):
    scale = (values.shape[1] // BLOCK / bin_count) ** (-0.5)
    return jnp.dot(values, matrix, preferred_element_type=jnp.float32) * scale


def gather_weights(value_w, output_w):
    return (
        lax.all_gather(value_w, "dp", axis=0, tiled=True),
        lax.all_gather(output_w, "dp", axis=1, tiled=True),
    )


def chain_step(current, inputs_bf, inv_rms, values, gain_row, value_full, output_full):
    dvalues = lax.dot_general(
        current, output_full, (((1,), (1,)), ((), ())), preferred_element_type=jnp.float32
    ).astype(jnp.bfloat16)
    row_sum = jnp.sum(dvalues.astype(jnp.float32) * values, axis=-1, keepdims=True)
    dhidden = lax.dot_general(
        dvalues, value_full, (((1,), (1,)), ((), ())), preferred_element_type=jnp.float32
    )
    coef = row_sum * inv_rms * inv_rms / inputs_bf.shape[1]
    grad_next = (
        current.astype(jnp.float32)
        + dhidden * gain_row * inv_rms
        - inputs_bf.astype(jnp.float32) * coef
    ).astype(jnp.bfloat16)
    return dvalues, grad_next


def body(acts, cotangent, gains, value_w, output_w, d_map, r_map, lengths, item_panels, owners):
    section_count = lax.axis_size("section")
    section_id = lax.axis_index("section")
    last_section = section_count - 1
    owner_count = lax.axis_size("dp")
    dp_id = lax.axis_index("dp")
    doc_count = lengths.shape[0]
    inputs_bf = acts[0]
    token_count, model_width = inputs_bf.shape
    slot_count = token_count // doc_count
    feature_width = item_panels.shape[2] * item_panels.shape[3] * item_panels.shape[4]

    value_full, output_full = gather_weights(value_w[0], output_w[0])

    own_panels = item_panels[:, 0].reshape(item_panels.shape[0], feature_width)
    per_owner = own_panels.shape[0]
    panels = [own_panels]
    for distance in range(1, owner_count):
        route = [(i, (i + distance) % owner_count) for i in range(owner_count)]
        panels.append(lax.ppermute(own_panels, "dp", route))
    all_rows = jnp.concatenate(panels, axis=0)

    gain_row = gains
    inputs = inputs_bf.astype(jnp.float32)
    inv_rms = lax.rsqrt(jnp.mean(inputs * inputs, axis=-1, keepdims=True) + EPS)
    hidden = (inputs * inv_rms * gain_row).astype(jnp.bfloat16)
    model_matrix = projection(d_map[0], DBINS)
    value_matrix = projection(r_map[0], RBINS)
    hidden_proj = project_rows(hidden, model_matrix, DBINS)
    values = jnp.dot(hidden, value_full, preferred_element_type=jnp.float32)
    value_proj = project_rows(values.astype(jnp.bfloat16), value_matrix, RBINS)

    positions = jnp.arange(slot_count, dtype=jnp.int32)
    live_mask = (positions[None, :] < lengths[:, None]).reshape(token_count, 1)
    current = jnp.where(live_mask, cotangent, jnp.zeros_like(cotangent))

    for turn in range(section_count):
        dvalues, grad_next = chain_step(
            current, inputs_bf, inv_rms, values, gain_row, value_full, output_full
        )
        if turn < last_section:
            source = last_section - turn
            incoming = lax.ppermute(grad_next, "section", [(source, source - 1)])
            current = jnp.where(section_id == source - 1, incoming, current)

    dvalue_proj = project_rows(dvalues, value_matrix, RBINS)
    grad_proj = project_rows(current, model_matrix, DBINS)

    def by_doc(rows):
        return rows.reshape(doc_count, slot_count, rows.shape[1])

    def feature(left, right):
        return jnp.einsum(
            "dtk,dtj->dkj", by_doc(left), by_doc(right), precision=lax.Precision.HIGHEST
        )

    inverse_len = 1.0 / lengths.astype(jnp.float32)
    features = jnp.stack(
        [feature(hidden_proj, dvalue_proj), feature(grad_proj, value_proj)], axis=1
    )
    features = (features * inverse_len[:, None, None, None]).astype(jnp.bfloat16)
    features = features.reshape(doc_count, feature_width)
    products = lax.dot_general(
        features, all_rows, (((1,), (1,)), ((), ())), preferred_element_type=jnp.float32
    )
    places = jnp.mod(dp_id - owners, owner_count)
    collected = jnp.take(
        products.reshape(doc_count, owner_count, per_owner), places, axis=1
    ).reshape(doc_count, owner_count * per_owner)
    scores = lax.psum(collected * (feature_width // 2) ** (-0.5), "section")
    return (grad_next[None], scores)


def solution(mesh):
    in_specs = (
        P("section", "dp", None),
        P("dp", None),
        P("section", None),
        P("section", "dp", None),
        P("section", None, "dp"),
        P("section", None),
        P("section", None),
        P("dp"),
        P("dp", "section", None, None, None),
        P(),
    )
    out_specs = (P("section", "dp", None), P("dp", None))
    return jax.shard_map(body, mesh=mesh, in_specs=in_specs, out_specs=out_specs, check_vma=False)
```

time: 612 us -> 444 us (0.73)
  waiting for transfers between devices: 454 us -> 266 us
  matrix products: 30.7 us -> 91.6 us
  local copies, waits for them, and re-layouts: 41.7 us -> 8.81 us
  blocking collectives: 48.3 us -> 26.4 us
  starting transfers between devices: 5.2 us -> 18 us
  other arithmetic: 17.7 us -> 11.4 us
    ppermute x4 -> x10, waiting for transfers between devices: 235 us -> 20.5 us  [the longest x3 19.6 us: body(): incoming = lax.ppermute(grad_next, 'section', [(source, source - 1)])]
    dot_general x9 -> x15, matrix products: 28.6 us -> 91.1 us  [the longest x4 43.8 us: chain_step(): lax.dot_general(dvalues, value_full, (((1,), (1,)), ((), ())), preferred_...]
    all_gather x1 -> x0, blocking collectives: 40.6 us -> none  [body(): all_rows = lax.all_gather(own_panels, 'dp', axis=0, tiled=True)]
    all_gather x2, waiting for transfers between devices: 217 us -> 245 us  [the longest x1 126 us: gather_weights(): lax.all_gather(output_w, 'dp', axis=1, tiled=True)]
    psum x1, blocking collectives: 7.64 us -> 26.4 us  [body(): scores = lax.psum(collected * (feature_width // 2) ** (-0.5), 'section')]
    ppermute x4 -> x10, starting transfers between devices: 5.12 us -> 18 us  [the longest x7 11.5 us: body(): panels.append(lax.ppermute(own_panels, 'dp', route))]
    another operation x6 -> x3, local copies, waits for them, and re-layouts: 10.3 us -> 0.18 us  [the longest x2 0.15 us: projection(): row_codes = jnp.repeat(codes, BLOCK)[:, None]]
    cond x17 -> x0, local copies, waits for them, and re-layouts: 7.48 us -> none
  transfers between devices with their start and end apart: 6 -> 12, of which waited for: 6 -> 4; matrix products, arithmetic and copies ran while one was open for 1% -> 6% of each run, Pallas kernels for 0% -> 0%
where the time goes in v1:
time: 444 us; the launch traced here: 438 us
  waiting for transfers between devices  266 us (60%)
  matrix products  91.6 us (21%)
  blocking collectives  26.4 us (6%)
  starting transfers between devices  18 us (4%)
  between operations  15.1 us (3%)
  other arithmetic  11.4 us (3%)
  local copies, waits for them, and re-layouts  8.81 us (2%)
    all_gather x1, waiting for transfers between devices, gather_weights(): lax.all_gather(output_w, 'dp', axis=1, tiled=True)  126 us
    all_gather x1, waiting for transfers between devices, gather_weights(): lax.all_gather(value_w, 'dp', axis=0, tiled=True)  118 us
    dot_general x4, matrix products, chain_step(): lax.dot_general(dvalues, value_full, (((1,), (1,)), ((), ())), preferred_...  43.8 us
    psum x1, blocking collectives, body(): scores = lax.psum(collected * (feature_width // 2) ** (-0.5), 'section')  26.4 us
    dot_general x4, matrix products, chain_step(): lax.dot_general(current, output_full, (((1,), (1,)), ((), ())), preferred...  25.5 us
    ppermute x3, waiting for transfers between devices, body(): incoming = lax.ppermute(grad_next, 'section', [(source, source - 1)])  19.6 us
    dot_general x4, matrix products, project_rows(): return jnp.dot(values, matrix, preferred_element_type=jnp.float32) * scale  11.5 us
    ppermute x7, starting transfers between devices, body(): panels.append(lax.ppermute(own_panels, 'dp', route))  11.5 us
  transfers between devices with their start and end apart: 12, of which 4 were waited for; matrix products, arithmetic and copies ran while one was open for 6% of the time, Pallas kernels for 0%

profile of v1, /device:TPU:0, one launch (start us, length us, event | category | flops | bytes accessed | tf_op | source)
XLA Modules:
  0.0 437.8 jit_solution(17814409003967722004)
XLA Ops:
  9.4 2.6 fusion.18
  12.0 126.2 %all-gather.5.cloned.1.call-done = bf16[1,1024,4096]{2,1,0:T(8,128)(2,1)} async-done(((bf16[1,1024,512]{2,1,0:T(8,128)(2,1)}), bf16[1,1024,4096]{2,1,0:T(8,128)(2,1)}) %all-gather.5.cloned.1.call-update) | async-done | bytes 8388624 | tf_op jit(solution)/shard_map/all_gather | solution.py:31
  138.2 6.9 %fusion.41 = bf16[384,1024]{1,0:T(8,128)(2,1)} fusion(bf16[1,1024,4096]{2,1,0:T(8,128)(2,1)} %all-gather.5.cloned.1.call-done, bf16[384,4096]{1,0:T(8,128)(2,1)S(1)} %copy-done.2, pred[384]{0:T(512)(128)(4,1)S(1)} %fusion.81), kind=kOutput, calls=%fused_computation.49 | convolution fusion | flops 3223191552 | bytes 12321152 | tf_op jit(solution)/shard_map/dot_general | solution.py:36
  145.1 118.4 %all-gather.7.cloned.1.call-done = bf16[1,4096,1024]{2,1,0:T(8,128)(2,1)} async-done(((bf16[1,512,1024]{2,1,0:T(8,128)(2,1)}), bf16[1,4096,1024]{2,1,0:T(8,128)(2,1)}) %all-gather.7.cloned.1.call-update) | async-done | bytes 8388624 | tf_op jit(solution)/shard_map/all_gather | solution.py:30
  263.5 9.2 %multiply_reduce_fusion.3 = (f32[384]{0:T(512)S(1)}, f32[384,1024]{1,0:T(8,128)}) fusion(bf16[384,1024]{1,0:T(8,128)(2,1)} %fusion.41, bf16[1,4096,1024]{2,1,0:T(8,128)(2,1)} %all-gather.7.cloned.1.call-done, bf16[1,384,4096]{2,1,0:T(8,128)(2,1)} %param.10, f32[384]{0:T(512)S(1)} %add_rsqrt_fusion, f32[4096]{0:T(1024)S(1)} %bitcast.120), kind=kOutput, calls=%fused_computation.48 | convolution fusion | flops 3228696064 | bytes 13913088 | tf_op jit(solution)/shard_map/dot_general | solution.py:81
  272.7 11.0 %fusion.22 = bf16[384,4096]{1,0:T(8,128)(2,1)} fusion(bf16[384,1024]{1,0:T(8,128)(2,1)S(1)} %copy-done.43, bf16[1,4096,1024]{2,1,0:T(8,128)(2,1)} %all-gather.7.cloned.1.call-done, bf16[1,384,4096]{2,1,0:T(8,128)(2,1)S(1)} %copy-done.3, f32[384]{0:T(512)S(1)} %fusion.77, f32[384]{0:T(512)S(1)} %add_rsqrt_fusion, f32[4096]{0:T(1024)S(1)} %bitcast.121, ...), kind=kOutput, calls=%fused_computation.29 | convolution fusion | flops 3235381248 | bytes 18632064 | tf_op jit(solution)/shard_map/dot_general | solution.py:40
  283.7 2.8 collective-permute-start
  286.6 2.4 broadcast_select_fusion.1
  289.0 7.1 %multiply_reduce_fusion.2 = (f32[384]{0:T(512)S(1)}, bf16[384,1024]{1,0:T(8,128)(2,1)S(1)}) fusion(f32[384,1024]{1,0:T(8,128)S(1)} %copy-done.39, bf16[384,4096]{1,0:T(8,128)(2,1)S(1)} %broadcast_select_fusion.1, bf16[1,1024,4096]{2,1,0:T(8,128)(2,1)} %all-gather.5.cloned.1.call-done), kind=kOutput, calls=%fused_computation.47 | convolution fusion | flops 3222797824 | bytes 13895168 | tf_op jit(solution)/shard_map/dot_general | solution.py:36
  296.1 11.2 %fusion.24 = bf16[384,4096]{1,0:T(8,128)(2,1)} fusion(bf16[384,4096]{1,0:T(8,128)(2,1)S(1)} %broadcast_select_fusion.1, bf16[384,1024]{1,0:T(8,128)(2,1)S(1)} %get-tuple-element.15, bf16[1,4096,1024]{2,1,0:T(8,128)(2,1)} %all-gather.7.cloned.1.call-done, bf16[1,384,4096]{2,1,0:T(8,128)(2,1)S(1)} %copy-done.4, f32[384]{0:T(512)S(1)} %fusion.78, ...), kind=kOutput, calls=%fused_computation.31 | convolution fusion | flops 3233808384 | bytes 18631680 | tf_op jit(solution)/shard_map/dot_general | solution.py:40
  307.3 2.4 collective-permute-start.1
  311.1 8.1 %multiply_reduce_fusion.1 = (f32[384]{0:T(512)S(1)}, bf16[384,1024]{1,0:T(8,128)(2,1)S(1)}) fusion(f32[384,1024]{1,0:T(8,128)S(1)} %copy-done.40, bf16[384,4096]{1,0:T(8,128)(2,1)S(1)} %broadcast_select_fusion.2, bf16[1,1024,4096]{2,1,0:T(8,128)(2,1)} %all-gather.5.cloned.1.call-done), kind=kOutput, calls=%fused_computation.46 | convolution fusion | flops 3222797824 | bytes 13895168 | tf_op jit(solution)/shard_map/dot_general | solution.py:36
  319.3 11.2 %fusion.26 = bf16[384,4096]{1,0:T(8,128)(2,1)} fusion(bf16[384,4096]{1,0:T(8,128)(2,1)S(1)} %broadcast_select_fusion.2, bf16[384,1024]{1,0:T(8,128)(2,1)S(1)} %get-tuple-element.17, bf16[1,4096,1024]{2,1,0:T(8,128)(2,1)} %all-gather.7.cloned.1.call-done, bf16[1,384,4096]{2,1,0:T(8,128)(2,1)S(1)} %copy-done.5, f32[384]{0:T(512)S(1)} %fusion.79, ...), kind=kOutput, calls=%fused_computation.33 | convolution fusion | flops 3233808384 | bytes 18631680 | tf_op jit(solution)/shard_map/dot_general | solution.py:40
  332.6 2.9 collective-permute-start.5
  340.0 3.8 convolution_multiply_fusion.3
  344.9 2.6 collective-permute-start.8
  347.5 2.6 collective-permute-start.9
  352.7 3.8 concatenate.3
  356.5 3.7 convolution_multiply_fusion
  360.3 19.6 %collective-permute-done.2 = bf16[384,4096]{1,0:T(8,128)(2,1)} collective-permute-done((bf16[384,4096]{1,0:T(8,128)(2,1)}, bf16[384,4096]{1,0:T(8,128)(2,1)}, u32[]{:S(2)}, u32[]{:S(2)}) %collective-permute-start.2) | collective-permute-done | bytes 3145760 | tf_op jit(solution)/shard_map/ppermute | solution.py:94
  382.5 3.0 convolution_multiply_fusion.2
  386.4 3.5 multiply_reduce_fusion
  393.3 26.4 %psum.7 = f32[3,8]{0,1:T(8,128)S(1)} all-reduce(f32[3,8]{0,1:T(8,128)S(1)} %multiply_bitcast_fusion), channel_id=1, replica_groups=mesh['section'=4,'dp'=8] {'section'}, use_global_device_ids=true, to_apply=%region_5.6 | all-reduce | flops 24 | bytes 192 | tf_op jit(solution)/shard_map/psum | solution.py:121
  420.4 10.3 %fusion.37 = bf16[1,384,4096]{2,1,0:T(8,128)(2,1)} fusion(bf16[384,1024]{1,0:T(8,128)(2,1)} %copy-done.42, bf16[1,4096,1024]{2,1,0:T(8,128)(2,1)} %all-gather.7.cloned.1.call-done, bf16[384,4096]{1,0:T(8,128)(2,1)} %copy-done.7, bf16[1,384,4096]{2,1,0:T(8,128)(2,1)S(1)} %copy-done.6, f32[384]{0:T(512)S(1)} %fusion.80, f32[384]{0:T(512)S(1)} %copy-done.17, ...), kind=kOutput, calls=%fused_computation.36 | convolution fusion | flops 3233808384 | bytes 18631680 | tf_op jit(solution)/shard_map/dot_general | solution.py:40
  (147 shorter events, 21.0 us)
Async XLA Ops:
  7.2 131.0 %copy-start.2 = (bf16[384,4096]{1,0:T(8,128)(2,1)S(1)}, bf16[384,4096]{1,0:T(8,128)(2,1)}, u32[]{:S(2)}) copy-start(bf16[384,4096]{1,0:T(8,128)(2,1)} %param.11) | copy-start | bytes 9437188
  7.2 131.0 %all-gather.5.cloned.1.call-start = ((), (), s32[]{:S(2)}) async-start(), calls=%async_computation | async-start | bytes 9437184 | tf_op jit(solution)/shard_map/all_gather | solution.py:31
  7.9 255.6 %all-gather.7.cloned.1.call-start = ((), (), s32[]{:S(2)}) async-start(), calls=%async_computation.1 | async-start | bytes 9437184 | tf_op jit(solution)/shard_map/all_gather | solution.py:30
  12.0 307.3 %copy-start.16 = (f32[384]{0:T(512)}, f32[384]{0:T(512)S(1)}, u32[]{:S(2)}) copy-start(f32[384]{0:T(512)S(1)} %add_rsqrt_fusion) | copy-start | bytes 4612
  12.0 251.5 %copy-start.23 = (f32[1,4096]{1,0:T(1,128)S(1)}, f32[1,4096]{1,0:T(1,128)}, u32[]{:S(2)}) copy-start(f32[1,4096]{1,0:T(1,128)} %param.12) | copy-start | bytes 49156
  283.7 2.8 collective-permute-start
  307.3 2.5 collective-permute-start.1
  330.6 49.4 %collective-permute-start.2 = (bf16[384,4096]{1,0:T(8,128)(2,1)}, bf16[384,4096]{1,0:T(8,128)(2,1)}, u32[]{:S(2)}, u32[]{:S(2)}) collective-permute-start(bf16[384,4096]{1,0:T(8,128)(2,1)} %fusion.26), channel_id=1, source_target_pairs={{8,0},{9,1},{10,2},{11,3},{12,4},{13,5},{14,6},{15,7}} | collective-permute-start | bytes 9437192 | tf_op jit(solution)/shard_map/ppermute | solution.py:94
  332.0 11.9 %collective-permute-start.3 = (bf16[1,32768]{1,0:T(2,128)(2,1)S(1)}, bf16[1,32768]{1,0:T(2,128)(2,1)}, u32[]{:S(2)}, u32[]{:S(2)}) collective-permute-start(bf16[1,32768]{1,0:T(2,128)(2,1)S(1)} %bitcast.102), channel_id=1, source_target_pairs={{0,1},{1,2},{2,3},{3,4},{4,5},{5,6},{6,7},{7,0},{8,9},{9,10},{10,1... | collective-permute-start | bytes 196616 | tf_op jit(solution)/shard_map/ppermute | solution.py:71
  332.6 12.4 %collective-permute-start.4 = (bf16[1,32768]{1,0:T(2,128)(2,1)S(1)}, bf16[1,32768]{1,0:T(2,128)(2,1)}, u32[]{:S(2)}, u32[]{:S(2)}) collective-permute-start(bf16[1,32768]{1,0:T(2,128)(2,1)S(1)} %bitcast.103), channel_id=1, source_target_pairs={{0,2},{1,3},{2,4},{3,5},{4,6},{5,7},{6,0},{7,1},{8,10},{9,11},{10,... | collective-permute-start | bytes 196616 | tf_op jit(solution)/shard_map/ppermute | solution.py:71
  332.6 14.9 %collective-permute-start.5 = (bf16[1,32768]{1,0:T(2,128)(2,1)S(1)}, bf16[1,32768]{1,0:T(2,128)(2,1)}, u32[]{:S(2)}, u32[]{:S(2)}) collective-permute-start(bf16[1,32768]{1,0:T(2,128)(2,1)S(1)} %bitcast.104), channel_id=1, source_target_pairs={{0,3},{1,4},{2,5},{3,6},{4,7},{5,0},{6,1},{7,2},{8,11},{9,12},{10,... | collective-permute-start | bytes 196616 | tf_op jit(solution)/shard_map/ppermute | solution.py:71
  335.4 15.2 %collective-permute-start.6 = (bf16[1,32768]{1,0:T(2,128)(2,1)S(1)}, bf16[1,32768]{1,0:T(2,128)(2,1)}, u32[]{:S(2)}, u32[]{:S(2)}) collective-permute-start(bf16[1,32768]{1,0:T(2,128)(2,1)S(1)} %bitcast.105), channel_id=1, source_target_pairs={{0,4},{1,5},{2,6},{3,7},{4,0},{5,1},{6,2},{7,3},{8,12},{9,13},{10,... | collective-permute-start | bytes 196616 | tf_op jit(solution)/shard_map/ppermute | solution.py:71
  343.9 36.1 %copy-start.1 = (bf16[384,4096]{1,0:T(8,128)(2,1)S(1)}, bf16[384,4096]{1,0:T(8,128)(2,1)}, u32[]{:S(2)}) copy-start(bf16[384,4096]{1,0:T(8,128)(2,1)} %copy-done) | copy-start | bytes 9437188
  343.9 6.7 %collective-permute-start.7 = (bf16[1,32768]{1,0:T(2,128)(2,1)S(1)}, bf16[1,32768]{1,0:T(2,128)(2,1)S(1)}, u32[]{:S(2)}, u32[]{:S(2)}) collective-permute-start(bf16[1,32768]{1,0:T(2,128)(2,1)S(1)} %bitcast.106), channel_id=1, source_target_pairs={{0,5},{1,6},{2,7},{3,0},{4,1},{5,2},{6,3},{7,4},{8,13},{9,14},{10,... | collective-permute-start | bytes 196616 | tf_op jit(solution)/shard_map/ppermute | solution.py:71
  344.9 5.7 %collective-permute-start.8 = (bf16[1,32768]{1,0:T(2,128)(2,1)S(1)}, bf16[1,32768]{1,0:T(2,128)(2,1)S(1)}, u32[]{:S(2)}, u32[]{:S(2)}) collective-permute-start(bf16[1,32768]{1,0:T(2,128)(2,1)S(1)} %bitcast.107), channel_id=1, source_target_pairs={{0,6},{1,7},{2,0},{3,1},{4,2},{5,3},{6,4},{7,5},{8,14},{9,15},{10,... | collective-permute-start | bytes 196616 | tf_op jit(solution)/shard_map/ppermute | solution.py:71
  347.5 5.3 %collective-permute-start.9 = (bf16[1,32768]{1,0:T(2,128)(2,1)S(1)}, bf16[1,32768]{1,0:T(2,128)(2,1)}, u32[]{:S(2)}, u32[]{:S(2)}) collective-permute-start(bf16[1,32768]{1,0:T(2,128)(2,1)S(1)} %bitcast.108), channel_id=1, source_target_pairs={{0,7},{1,0},{2,1},{3,2},{4,3},{5,4},{6,5},{7,6},{8,15},{9,8},{10,9... | collective-permute-start | bytes 196616 | tf_op jit(solution)/shard_map/ppermute | solution.py:71
  360.3 22.1 %copy-start.15 = (pred[4096]{0:T(1024)(128)(4,1)S(1)}, pred[4096]{0:T(1024)(128)(4,1)}, u32[]{:S(2)}) copy-start(pred[4096]{0:T(1024)(128)(4,1)} %copy-done.14) | copy-start | bytes 12292
  360.3 22.1 %copy-start.28 = (pred[128]{0:T(512)(128)(4,1)S(1)}, pred[128]{0:T(512)(128)(4,1)}, u32[]{:S(2)}) copy-start(pred[128]{0:T(512)(128)(4,1)} %copy-done.27) | copy-start | bytes 388
  360.3 22.1 %copy-start.30 = (pred[128]{0:T(512)(128)(4,1)S(1)}, pred[128]{0:T(512)(128)(4,1)}, u32[]{:S(2)}) copy-start(pred[128]{0:T(512)(128)(4,1)} %copy-done.29) | copy-start | bytes 388
  360.3 22.1 %copy-start.32 = (s32[128]{0:T(128)S(1)}, s32[128]{0:T(128)}, u32[]{:S(2)}) copy-start(s32[128]{0:T(128)} %copy-done.31) | copy-start | bytes 1540
  360.3 22.1 %copy-start.34 = (s32[128]{0:T(128)S(1)}, s32[128]{0:T(128)}, u32[]{:S(2)}) copy-start(s32[128]{0:T(128)} %copy-done.33) | copy-start | bytes 1540
  389.9 30.5 %copy-start.6 = (bf16[1,384,4096]{2,1,0:T(8,128)(2,1)S(1)}, bf16[1,384,4096]{2,1,0:T(8,128)(2,1)}, u32[]{:S(2)}) copy-start(bf16[1,384,4096]{2,1,0:T(8,128)(2,1)} %param.10) | copy-start | bytes 9437188
  389.9 30.5 %copy-start.17 = (f32[384]{0:T(512)S(1)}, f32[384]{0:T(512)}, u32[]{:S(2)}) copy-start(f32[384]{0:T(512)} %copy-done.16) | copy-start | bytes 4612
  389.9 30.5 %copy-start.24 = (f32[1,4096]{1,0:T(1,128)S(1)}, f32[1,4096]{1,0:T(1,128)}, u32[]{:S(2)}) copy-start(f32[1,4096]{1,0:T(1,128)} %param.12) | copy-start | bytes 49156
  (34 other events, 259.4 us)
Sparse Core Ops, SparseCore 0:
  10.1 128.0 all-gather.4
  140.3 123.1 all-gather.6

commit v2 on v1

--- a/solution.py
+++ b/solution.py
@@ -1,6 +1,10 @@
+import functools
+
 import jax
 import jax.numpy as jnp
 from jax import lax
+from jax.experimental import pallas as pl
+from jax.experimental.pallas import tpu as pltpu
 from jax.sharding import PartitionSpec as P
 
 BLOCK = 64
@@ -25,11 +29,149 @@
     return jnp.dot(values, matrix, preferred_element_type=jnp.float32) * scale
 
 
+def gather_kernel(
+    line, value_ref, output_ref, value_full, output_full, local_sem, send_sem, recv_sem
+):
+    me = lax.axis_index("dp")
+    place = me // 2
+    side = me % 2
+    partner = place * 2 + (1 - side)
+    has_left = place > 0
+    has_right = place < line - 1
+    depth = value_ref.shape[0]
+    width = output_ref.shape[1]
+
+    barrier = pltpu.get_barrier_semaphore()
+
+    def greet(device):
+        pl.semaphore_signal(
+            barrier, inc=1, device_id={"dp": device}, device_id_type=pl.DeviceIdType.MESH
+        )
+
+    greet(partner)
+
+    @pl.when(has_left)
+    def _():
+        greet(me - 2)
+
+    @pl.when(has_right)
+    def _():
+        greet(me + 2)
+
+    peers = 1 + has_left.astype(jnp.int32) + has_right.astype(jnp.int32)
+    pl.semaphore_wait(barrier, peers)
+
+    def slot(weight, block):
+        if weight == 0:
+            if len(output_full.shape) == 3:
+                return output_full.at[block]
+            return output_full.at[:, pl.ds(pl.multiple_of(block * width, width), width)]
+        return value_full.at[pl.ds(pl.multiple_of(block * depth, depth), depth), :]
+
+    def copy(weight, block, device, way, own):
+        source = (output_ref, value_ref)[weight] if own else slot(weight, block)
+        return pltpu.make_async_remote_copy(
+            src_ref=source,
+            dst_ref=slot(weight, block),
+            send_sem=send_sem.at[weight, way, block // 2],
+            recv_sem=recv_sem.at[weight, block],
+            device_id={"dp": device},
+            device_id_type=pl.DeviceIdType.MESH,
+        )
+
+    def local(weight):
+        return pltpu.make_async_copy(
+            (output_ref, value_ref)[weight], slot(weight, me), local_sem.at[weight]
+        )
+
+    for weight in range(2):
+
+        @pl.when(has_left)
+        def _():
+            copy(weight, me, me - 2, 0, True).start()
+
+        @pl.when(has_right)
+        def _():
+            copy(weight, me, me + 2, 1, True).start()
+
+        copy(weight, me, partner, 2, True).start()
+        local(weight).start()
+
+    def relay(step, carry):
+        for weight in range(2):
+            from_left = me - 2 * step
+            from_right = me + 2 * step
+
+            @pl.when(place + step < line)
+            def _():
+                copy(weight, from_right, partner, 2, False).wait_recv()
+
+                @pl.when(has_left)
+                def _():
+                    copy(weight, from_right, me - 2, 0, False).start()
+
+                copy(weight, from_right, partner, 2, False).start()
+
+            @pl.when(place - step >= 0)
+            def _():
+                copy(weight, from_left, partner, 2, False).wait_recv()
+
+                @pl.when(has_right)
+                def _():
+                    copy(weight, from_left, me + 2, 1, False).start()
+
+                copy(weight, from_left, partner, 2, False).start()
+
+        return carry
+
+    lax.fori_loop(1, line, relay, 0)
+
+    def finish(index, carry):
+        for weight in range(2):
+            mine = index * 2 + side
+            copy(weight, index * 2 + (1 - side), partner, 2, False).wait_recv()
+            copy(weight, mine, partner, 2, False).wait_send()
+
+            @pl.when(has_left & (index >= place))
+            def _():
+                copy(weight, mine, partner, 0, False).wait_send()
+
+            @pl.when(has_right & (index <= place))
+            def _():
+                copy(weight, mine, partner, 1, False).wait_send()
+
+        return carry
+
+    lax.fori_loop(0, line, finish, 0)
+    for weight in range(2):
+        local(weight).wait()
+
+
 def gather_weights(value_w, output_w):
-    return (
-        lax.all_gather(value_w, "dp", axis=0, tiled=True),
-        lax.all_gather(output_w, "dp", axis=1, tiled=True),
-    )
+    count = lax.axis_size("dp")
+    line = count // 2
+    rows, width = output_w.shape
+    aligned = width % 128 == 0
+    output_shape = (rows, width * count) if aligned else (count, rows, width)
+    value_full, output_full = pl.pallas_call(
+        functools.partial(gather_kernel, line),
+        out_shape=(
+            jax.ShapeDtypeStruct((value_w.shape[0] * count, value_w.shape[1]), value_w.dtype),
+            jax.ShapeDtypeStruct(output_shape, output_w.dtype),
+        ),
+        in_specs=[pl.BlockSpec(memory_space=pl.ANY)] * 2,
+        out_specs=(pl.BlockSpec(memory_space=pl.ANY), pl.BlockSpec(memory_space=pl.ANY)),
+        scratch_shapes=[
+            pltpu.SemaphoreType.DMA((2,)),
+            pltpu.SemaphoreType.DMA((2, 3, line)),
+            pltpu.SemaphoreType.DMA((2, count)),
+        ],
+        compiler_params=pltpu.CompilerParams(collective_id=0, has_side_effects=True),
+        name="gather_weights",
+    )(value_w, output_w)
+    if not aligned:
+        output_full = output_full.swapaxes(0, 1).reshape(rows, width * count)
+    return value_full, output_full
 
 
 def chain_step(current, inputs_bf, inv_rms, values, gain_row, value_full, output_full):

time: 444 us -> 367 us (0.83)
  waiting for transfers between devices: 266 us -> 21.2 us
  Pallas kernels: 0 us -> 185 us
  between operations: 15.1 us -> 1.76 us
    all_gather x2 -> x0, waiting for transfers between devices: 245 us -> none  [the longest x1 126 us: gather_weights(): lax.all_gather(output_w, 'dp', axis=1, tiled=True)]
    pallas_call x0 -> x1, Pallas kernels: none -> 185 us  [gather_weights(): pl.pallas_call(functools.partial(gather_kernel, line), out_shape=(jax.Sha...]
  transfers between devices with their start and end apart: 12 -> 10, of which waited for: 4 -> 3; matrix products, arithmetic and copies ran while one was open for 6% -> 4% of each run, Pallas kernels for 0% -> 0%
where the time goes in v2:
time: 367 us; the launch traced here: 361 us
  Pallas kernels  185 us (50%)
  matrix products  89.1 us (24%)
  blocking collectives  26 us (7%)
  waiting for transfers between devices  21.2 us (6%)
  starting transfers between devices  19.1 us (5%)
  other arithmetic  9.91 us (3%)
  local copies, waits for them, and re-layouts  8.4 us (2%)
    pallas_call x1, Pallas kernels, gather_weights(): pl.pallas_call(functools.partial(gather_kernel, line), out_shape=(jax.Sha...  185 us
    dot_general x4, matrix products, chain_step(): lax.dot_general(dvalues, value_full, (((1,), (1,)), ((), ())), preferred_...  43.9 us
    psum x1, blocking collectives, body(): scores = lax.psum(collected * (feature_width // 2) ** (-0.5), 'section')  26 us
    dot_general x4, matrix products, chain_step(): lax.dot_general(current, output_full, (((1,), (1,)), ((), ())), preferred...  24.8 us
    ppermute x3, waiting for transfers between devices, body(): incoming = lax.ppermute(grad_next, 'section', [(source, source - 1)])  20.1 us
    ppermute x7, starting transfers between devices, body(): panels.append(lax.ppermute(own_panels, 'dp', route))  12.6 us
    dot_general x4, matrix products, project_rows(): return jnp.dot(values, matrix, preferred_element_type=jnp.float32) * scale  10.8 us
    dot_general x1, matrix products, body(): values = jnp.dot(hidden, value_full, preferred_element_type=jnp.float32)  8.08 us
  transfers between devices with their start and end apart: 10, of which 3 were waited for; matrix products, arithmetic and copies ran while one was open for 4% of the time, Pallas kernels for 0%

profile of v2, /device:TPU:0, one launch (start us, length us, event | category | flops | bytes accessed | tf_op | source)
XLA Modules:
  0.0 361.0 jit_solution(6743092820776575922)
XLA Ops:
  0.7 2.7 fusion
  3.5 185.4 %gather_weights.1 = (bf16[4096,1024]{1,0:T(8,128)(2,1)}, bf16[1024,4096]{1,0:T(8,128)(2,1)}) custom-call(bf16[512,1024]{1,0:T(8,128)(2,1)} %bitcast.67, bf16[1024,512]{1,0:T(8,128)(2,1)} %bitcast.68), custom_call_target="tpu_custom_call" | custom-call | tf_op jit(solution)/shard_map/gather_weights/pallas_call | solution.py:156
  189.0 6.1 %convolution_convert_fusion.3 = bf16[384,1024]{1,0:T(8,128)(2,1)S(1)} fusion(bf16[1024,4096]{1,0:T(8,128)(2,1)} %get-tuple-element.4, bf16[384,4096]{1,0:T(8,128)(2,1)S(1)} %copy-done.2, pred[384]{0:T(512)(128)(4,1)S(1)} %fusion.42), kind=kOutput, calls=%fused_computation.34 | convolution fusion | flops 3223191552 | bytes 12321152 | tf_op jit(solution)/shard_map/dot_general | solution.py:178
  195.1 8.1 %multiply_reduce_fusion.3 = (f32[384]{0:T(512)S(1)}, f32[384,1024]{1,0:T(8,128)}) fusion(bf16[384,1024]{1,0:T(8,128)(2,1)S(1)} %convolution_convert_fusion.3, bf16[4096,1024]{1,0:T(8,128)(2,1)} %get-tuple-element.5, bf16[1,384,4096]{2,1,0:T(8,128)(2,1)S(1)} %copy-done.3, f32[384]{0:T(512)S(1)} %add_rsqrt_fusion, f32[4096]{0:T(1024)S(1)} %bitcast.87), kind=kOutput, calls=%fused_computation.30 | convolution fusion | flops 3228696064 | bytes 13913088 | tf_op jit(solution)/shard_map/dot_general | solution.py:223
  203.2 11.0 %fusion.4 = bf16[384,4096]{1,0:T(8,128)(2,1)} fusion(bf16[384,1024]{1,0:T(8,128)(2,1)S(1)} %convolution_convert_fusion.3, bf16[4096,1024]{1,0:T(8,128)(2,1)} %get-tuple-element.5, bf16[1,384,4096]{2,1,0:T(8,128)(2,1)S(1)} %copy-done.3, f32[384]{0:T(512)S(1)} %fusion.38, f32[384]{0:T(512)S(1)} %add_rsqrt_fusion, f32[4096]{0:T(1024)S(1)} %bitcast.88, ...), kind=kOutput, calls=%fused_computation.11 | convolution fusion | flops 3235381248 | bytes 18632064 | tf_op jit(solution)/shard_map/dot_general | solution.py:182
  214.3 2.8 collective-permute-start
  217.1 2.4 broadcast_select_fusion.1
  219.5 7.0 %multiply_reduce_fusion.2 = (f32[384]{0:T(512)S(1)}, bf16[384,1024]{1,0:T(8,128)(2,1)S(1)}) fusion(f32[384,1024]{1,0:T(8,128)S(1)} %copy-done.44, bf16[384,4096]{1,0:T(8,128)(2,1)S(1)} %broadcast_select_fusion.1, bf16[1024,4096]{1,0:T(8,128)(2,1)} %get-tuple-element.4), kind=kOutput, calls=%fused_computation.29 | convolution fusion | flops 3222797824 | bytes 13895168 | tf_op jit(solution)/shard_map/dot_general | solution.py:178
  226.6 11.2 %fusion.6 = bf16[384,4096]{1,0:T(8,128)(2,1)} fusion(bf16[384,4096]{1,0:T(8,128)(2,1)S(1)} %broadcast_select_fusion.1, bf16[384,1024]{1,0:T(8,128)(2,1)S(1)} %get-tuple-element.19, bf16[4096,1024]{1,0:T(8,128)(2,1)} %get-tuple-element.5, bf16[1,384,4096]{2,1,0:T(8,128)(2,1)S(1)} %copy-done.4, f32[384]{0:T(512)S(1)} %fusion.39, f32[384]{0:T(512)S(1)} %add_rsqrt_fusion, ...), kind=kOutput, calls=%fused_computation.13 | convolution fusion | flops 3233808384 | bytes 18631680 | tf_op jit(solution)/shard_map/dot_general | solution.py:182
  237.8 2.4 collective-permute-start.1
  241.7 8.1 %multiply_reduce_fusion.1 = (f32[384]{0:T(512)S(1)}, bf16[384,1024]{1,0:T(8,128)(2,1)S(1)}) fusion(f32[384,1024]{1,0:T(8,128)S(1)} %copy-done.45, bf16[384,4096]{1,0:T(8,128)(2,1)S(1)} %broadcast_select_fusion.2, bf16[1024,4096]{1,0:T(8,128)(2,1)} %get-tuple-element.4), kind=kOutput, calls=%fused_computation.28 | convolution fusion | flops 3222797824 | bytes 13895168 | tf_op jit(solution)/shard_map/dot_general | solution.py:178
  249.9 11.3 %fusion.8 = bf16[384,4096]{1,0:T(8,128)(2,1)} fusion(bf16[384,4096]{1,0:T(8,128)(2,1)S(1)} %broadcast_select_fusion.2, bf16[384,1024]{1,0:T(8,128)(2,1)S(1)} %get-tuple-element.21, bf16[4096,1024]{1,0:T(8,128)(2,1)} %get-tuple-element.5, bf16[1,384,4096]{2,1,0:T(8,128)(2,1)S(1)} %copy-done.5, f32[384]{0:T(512)S(1)} %fusion.40, f32[384]{0:T(512)S(1)} %add_rsqrt_fusion, ...), kind=kOutput, calls=%fused_computation.15 | convolution fusion | flops 3233808384 | bytes 18631680 | tf_op jit(solution)/shard_map/dot_general | solution.py:182
  263.2 1.6 collective-permute-start.4
  264.8 2.5 collective-permute-start.5
  267.3 2.3 collective-permute-start.6
  271.7 5.8 %convolution_multiply_fusion.3 = f32[384,128]{1,0:T(8,128)} fusion(bf16[1,384,4096]{2,1,0:T(8,128)(2,1)} %param.10, f32[384]{0:T(512)} %copy-done.19, f32[4096]{0:T(1024)} %bitcast.86, s32[4096]{0:T(1024)S(1)} %get-tuple-element.13, s32[128]{0:T(128)S(1)} %get-tuple-element.28, s32[128]{0:T(128)S(1)} %get-tuple-element.30, s32[4096]{0:T(1024)S(1)} %get-tuple-element.12, ...), kind=kOutput, calls=%fused_computation.40 | convolution fusion | flops 413188096 | bytes 3432192 | tf_op jit(solution)/shard_map/dot_general | solution.py:29
  281.2 2.6 collective-permute-start.9
  286.4 3.8 %concatenate.3 = bf16[8,32768]{1,0:T(8,128)(2,1)} concatenate(bf16[1,32768]{1,0:T(2,128)(2,1)S(1)} %bitcast.76, bf16[1,32768]{1,0:T(2,128)(2,1)} %collective-permute-done.3, bf16[1,32768]{1,0:T(2,128)(2,1)} %collective-permute-done.4, bf16[1,32768]{1,0:T(2,128)(2,1)} %collective-permute-done.5, bf16[1,32768]{1,0:T(2,128)(2,1)} %collective-permute-done.6, ...), dimensions={0} | concatenate | bytes 1048576 | tf_op jit(solution)/shard_map/concatenate | solution.py:214
  290.3 20.1 %collective-permute-done.2 = bf16[384,4096]{1,0:T(8,128)(2,1)} collective-permute-done((bf16[384,4096]{1,0:T(8,128)(2,1)}, bf16[384,4096]{1,0:T(8,128)(2,1)}, u32[]{:S(2)}, u32[]{:S(2)}) %collective-permute-start.2) | collective-permute-done | bytes 3145760 | tf_op jit(solution)/shard_map/ppermute | solution.py:236
  310.4 2.4 broadcast_select_fusion.3
  312.8 3.0 convolution_multiply_fusion.2
  316.7 3.5 multiply_reduce_fusion
  323.7 26.0 %psum.7 = f32[3,8]{0,1:T(8,128)S(1)} all-reduce(f32[3,8]{0,1:T(8,128)S(1)} %multiply_bitcast_fusion), channel_id=1, replica_groups=mesh['section'=4,'dp'=8] {'section'}, use_global_device_ids=true, to_apply=%region_5.6 | all-reduce | flops 24 | bytes 192 | tf_op jit(solution)/shard_map/psum | solution.py:263
  350.4 10.3 %fusion.11 = bf16[1,384,4096]{2,1,0:T(8,128)(2,1)} fusion(bf16[384,1024]{1,0:T(8,128)(2,1)} %copy-done.48, bf16[4096,1024]{1,0:T(8,128)(2,1)} %get-tuple-element.5, bf16[384,4096]{1,0:T(8,128)(2,1)} %copy-done.7, bf16[1,384,4096]{2,1,0:T(8,128)(2,1)S(1)} %copy-done.6, f32[384]{0:T(512)S(1)} %fusion.41, f32[384]{0:T(512)S(1)} %copy-done.20, ...), kind=kOutput, calls=%fused_computation.18 | convolution fusion | flops 3233808384 | bytes 18631680 | tf_op jit(solution)/shard_map/dot_general | solution.py:182
  (150 shorter events, 16.5 us)
Async XLA Ops:
  0.6 188.3 %copy-start.2 = (bf16[384,4096]{1,0:T(8,128)(2,1)S(1)}, bf16[384,4096]{1,0:T(8,128)(2,1)}, u32[]{:S(2)}) copy-start(bf16[384,4096]{1,0:T(8,128)(2,1)} %param.11) | copy-start | bytes 9437188
  3.4 246.4 %copy-start.19 = (f32[384]{0:T(512)}, f32[384]{0:T(512)S(1)}, u32[]{:S(2)}) copy-start(f32[384]{0:T(512)S(1)} %add_rsqrt_fusion) | copy-start | bytes 4612
  214.3 2.8 collective-permute-start
  237.8 2.5 collective-permute-start.1
  249.9 20.8 %copy-start.46 = (f32[384,1024]{1,0:T(8,128)S(1)}, f32[384,1024]{1,0:T(8,128)}, u32[]{:S(2)}) copy-start(f32[384,1024]{1,0:T(8,128)} %get-tuple-element.17) | copy-start | bytes 4718596
  261.2 49.2 %collective-permute-start.2 = (bf16[384,4096]{1,0:T(8,128)(2,1)}, bf16[384,4096]{1,0:T(8,128)(2,1)}, u32[]{:S(2)}, u32[]{:S(2)}) collective-permute-start(bf16[384,4096]{1,0:T(8,128)(2,1)} %fusion.8), channel_id=1, source_target_pairs={{8,0},{9,1},{10,2},{11,3},{12,4},{13,5},{14,6},{15,7}} | collective-permute-start | bytes 9437192 | tf_op jit(solution)/shard_map/ppermute | solution.py:236
  262.6 15.5 %collective-permute-start.3 = (bf16[1,32768]{1,0:T(2,128)(2,1)S(1)}, bf16[1,32768]{1,0:T(2,128)(2,1)}, u32[]{:S(2)}, u32[]{:S(2)}) collective-permute-start(bf16[1,32768]{1,0:T(2,128)(2,1)S(1)} %bitcast.69), channel_id=1, source_target_pairs={{0,1},{1,2},{2,3},{3,4},{4,5},{5,6},{6,7},{7,0},{8,9},{9,10},{10,1... | collective-permute-start | bytes 196616 | tf_op jit(solution)/shard_map/ppermute | solution.py:213
  263.2 16.5 %collective-permute-start.4 = (bf16[1,32768]{1,0:T(2,128)(2,1)S(1)}, bf16[1,32768]{1,0:T(2,128)(2,1)}, u32[]{:S(2)}, u32[]{:S(2)}) collective-permute-start(bf16[1,32768]{1,0:T(2,128)(2,1)S(1)} %bitcast.70), channel_id=1, source_target_pairs={{0,2},{1,3},{2,4},{3,5},{4,6},{5,7},{6,0},{7,1},{8,10},{9,11},{10,... | collective-permute-start | bytes 196616 | tf_op jit(solution)/shard_map/ppermute | solution.py:213
  264.8 16.4 %collective-permute-start.5 = (bf16[1,32768]{1,0:T(2,128)(2,1)S(1)}, bf16[1,32768]{1,0:T(2,128)(2,1)}, u32[]{:S(2)}, u32[]{:S(2)}) collective-permute-start(bf16[1,32768]{1,0:T(2,128)(2,1)S(1)} %bitcast.71), channel_id=1, source_target_pairs={{0,3},{1,4},{2,5},{3,6},{4,7},{5,0},{6,1},{7,2},{8,11},{9,12},{10,... | collective-permute-start | bytes 196616 | tf_op jit(solution)/shard_map/ppermute | solution.py:213
  267.3 17.2 %collective-permute-start.6 = (bf16[1,32768]{1,0:T(2,128)(2,1)S(1)}, bf16[1,32768]{1,0:T(2,128)(2,1)}, u32[]{:S(2)}, u32[]{:S(2)}) collective-permute-start(bf16[1,32768]{1,0:T(2,128)(2,1)S(1)} %bitcast.72), channel_id=1, source_target_pairs={{0,4},{1,5},{2,6},{3,7},{4,0},{5,1},{6,2},{7,3},{8,12},{9,13},{10,... | collective-permute-start | bytes 196616 | tf_op jit(solution)/shard_map/ppermute | solution.py:213
  271.7 38.7 %copy-start.1 = (bf16[384,4096]{1,0:T(8,128)(2,1)S(1)}, bf16[384,4096]{1,0:T(8,128)(2,1)}, u32[]{:S(2)}) copy-start(bf16[384,4096]{1,0:T(8,128)(2,1)} %copy-done) | copy-start | bytes 9437188
  278.1 6.3 %collective-permute-start.7 = (bf16[1,32768]{1,0:T(2,128)(2,1)S(1)}, bf16[1,32768]{1,0:T(2,128)(2,1)S(1)}, u32[]{:S(2)}, u32[]{:S(2)}) collective-permute-start(bf16[1,32768]{1,0:T(2,128)(2,1)S(1)} %bitcast.73), channel_id=1, source_target_pairs={{0,5},{1,6},{2,7},{3,0},{4,1},{5,2},{6,3},{7,4},{8,13},{9,14},{10,... | collective-permute-start | bytes 196616 | tf_op jit(solution)/shard_map/ppermute | solution.py:213
  279.7 5.2 %collective-permute-start.8 = (bf16[1,32768]{1,0:T(2,128)(2,1)S(1)}, bf16[1,32768]{1,0:T(2,128)(2,1)S(1)}, u32[]{:S(2)}, u32[]{:S(2)}) collective-permute-start(bf16[1,32768]{1,0:T(2,128)(2,1)S(1)} %bitcast.74), channel_id=1, source_target_pairs={{0,6},{1,7},{2,0},{3,1},{4,2},{5,3},{6,4},{7,5},{8,14},{9,15},{10,... | collective-permute-start | bytes 196616 | tf_op jit(solution)/shard_map/ppermute | solution.py:213
  281.2 5.3 %collective-permute-start.9 = (bf16[1,32768]{1,0:T(2,128)(2,1)S(1)}, bf16[1,32768]{1,0:T(2,128)(2,1)}, u32[]{:S(2)}, u32[]{:S(2)}) collective-permute-start(bf16[1,32768]{1,0:T(2,128)(2,1)S(1)} %bitcast.75), channel_id=1, source_target_pairs={{0,7},{1,0},{2,1},{3,2},{4,3},{5,4},{6,5},{7,6},{8,15},{9,8},{10,9... | collective-permute-start | bytes 196616 | tf_op jit(solution)/shard_map/ppermute | solution.py:213
  290.2 22.5 %copy-start.18 = (pred[4096]{0:T(1024)(128)(4,1)S(1)}, pred[4096]{0:T(1024)(128)(4,1)}, u32[]{:S(2)}) copy-start(pred[4096]{0:T(1024)(128)(4,1)} %copy-done.17) | copy-start | bytes 12292
  290.2 22.5 %copy-start.33 = (pred[128]{0:T(512)(128)(4,1)S(1)}, pred[128]{0:T(512)(128)(4,1)}, u32[]{:S(2)}) copy-start(pred[128]{0:T(512)(128)(4,1)} %copy-done.32) | copy-start | bytes 388
  290.2 22.5 %copy-start.35 = (pred[128]{0:T(512)(128)(4,1)S(1)}, pred[128]{0:T(512)(128)(4,1)}, u32[]{:S(2)}) copy-start(pred[128]{0:T(512)(128)(4,1)} %copy-done.34) | copy-start | bytes 388
  290.2 22.5 %copy-start.37 = (s32[128]{0:T(128)S(1)}, s32[128]{0:T(128)}, u32[]{:S(2)}) copy-start(s32[128]{0:T(128)} %copy-done.36) | copy-start | bytes 1540
  290.3 22.5 %copy-start.39 = (s32[128]{0:T(128)S(1)}, s32[128]{0:T(128)}, u32[]{:S(2)}) copy-start(s32[128]{0:T(128)} %copy-done.38) | copy-start | bytes 1540
  290.3 22.5 %copy-start.41 = (s32[128]{0:T(128)S(1)}, s32[128]{0:T(128)}, u32[]{:S(2)}) copy-start(s32[128]{0:T(128)} %copy-done.40) | copy-start | bytes 1540
  290.3 22.5 %copy-start.43 = (s32[128]{0:T(128)S(1)}, s32[128]{0:T(128)}, u32[]{:S(2)}) copy-start(s32[128]{0:T(128)} %copy-done.42) | copy-start | bytes 1540
  320.3 30.0 %copy-start.6 = (bf16[1,384,4096]{2,1,0:T(8,128)(2,1)S(1)}, bf16[1,384,4096]{2,1,0:T(8,128)(2,1)}, u32[]{:S(2)}) copy-start(bf16[1,384,4096]{2,1,0:T(8,128)(2,1)} %param.10) | copy-start | bytes 9437188
  320.3 30.0 %copy-start.20 = (f32[384]{0:T(512)S(1)}, f32[384]{0:T(512)}, u32[]{:S(2)}) copy-start(f32[384]{0:T(512)} %copy-done.19) | copy-start | bytes 4612
  320.3 30.0 %copy-start.27 = (f32[1,4096]{1,0:T(1,128)S(1)}, f32[1,4096]{1,0:T(1,128)}, u32[]{:S(2)}) copy-start(f32[1,4096]{1,0:T(1,128)} %param.12) | copy-start | bytes 49156
  (37 other events, 228.3 us)
